TPU v7x, 32 devices: a whole 2x2x4 slice. The times are simulated.
32 devices in a mesh: fsdp: 4 (over y, core), ctx: 4 (over z), tp: 2 (over x).
Axes of the slice: x: 2, y: 2, z: 4, core: 2. Of those that a mesh axis runs over, the one named last changes fastest.
Arguments:
- tokens: bfloat16 [8, 2048, 960], P('fsdp', ('ctx', 'tp')), may hold values from -6 to 6
- cotangent: bfloat16 [8, 2048, 960], P('fsdp', ('ctx', 'tp')), may hold values from -6 to 6
- input_gain: bfloat16 [960], P('fsdp'), may hold values from 0.099609375 to 1.8984375
- w_query: bfloat16 [960, 960], P('fsdp'), may hold values from -0.1875 to 0.1875
- w_keyval: bfloat16 [960, 640], P('fsdp'), may hold values from -0.1875 to 0.1875
- w_output: bfloat16 [960, 960], P('fsdp'), may hold values from -2 to 2
- middle_gain: bfloat16 [960], P('fsdp'), may hold values from 0.099609375 to 1.8984375
- w_gate: bfloat16 [960, 2560], P('fsdp', 'tp'), may hold values from -0.1875 to 0.1875
- w_up: bfloat16 [960, 2560], P('fsdp', 'tp'), may hold values from -0.1875 to 0.1875
- w_down: bfloat16 [960, 2560], P('fsdp', 'tp'), may hold values from -0.25 to 0.25
Outputs:
- result: bfloat16 [8, 2048, 960], P('fsdp', ('ctx', 'tp'))
- grad_tokens: float32 [8, 2048, 960], P('fsdp', ('ctx', 'tp'))
- grad_input_gain: float32 [960], P('fsdp')
- grad_w_query: float32 [960, 960], P('fsdp')
- grad_w_keyval: float32 [960, 640], P('fsdp')
- grad_w_output: float32 [960, 960], P('fsdp')
- grad_middle_gain: float32 [960], P('fsdp')
- grad_w_gate: float32 [960, 2560], P('fsdp', 'tp')
- grad_w_up: float32 [960, 2560], P('fsdp', 'tp')
- grad_w_down: float32 [960, 2560], P('fsdp', 'tp')
All inputs are finite; a program needn't handle non-finite values.
Results may differ from a plain program's by a relative error of at most 0.02.
Values may be sent and summed in bfloat16 or wider, within the bound.
A program may use at most 128 MiB of HBM per device.

v0:
```python
from functools import partial
import jax
import jax.numpy as jnp
from jax import lax
from jax.sharding import PartitionSpec as P

QUERY_HEADS = 15
KEYVAL_HEADS = 5
HEAD_WIDTH = 64
SEQUENCE_LENGTH = 2048
KEY_WIDTH = 320
EPS = 1e-05
THETA = 10000.0


def rope_tables(token_positions, first_place):
    half_width = HEAD_WIDTH // 2
    position = (first_place + lax.iota(jnp.int32, token_positions)).astype(jnp.float32)
    frequency = THETA ** (-(2.0 * lax.iota(jnp.int32, half_width).astype(jnp.float32)) / HEAD_WIDTH)
    angles = position[:, None] * frequency[None, :]
    return (jnp.cos(angles), jnp.sin(angles))


def apply_rotary(value_rows, cosine_table, sine_table, heads):
    half_width = HEAD_WIDTH // 2
    shaped = value_rows.reshape(value_rows.shape[:-1] + (heads, HEAD_WIDTH))
    leading = shaped[..., :half_width]
    trailing = shaped[..., half_width:]
    cosine_wide = cosine_table[:, None, :]
    sine_wide = sine_table[:, None, :]
    turned = jnp.concatenate(
        [
            leading * cosine_wide - trailing * sine_wide,
            trailing * cosine_wide + leading * sine_wide,
        ],
        -1,
    )
    return turned.reshape(value_rows.shape)


def normalize(value_rows):
    inverse_rms = lax.rsqrt(jnp.mean(value_rows * value_rows, -1, keepdims=True) + EPS)
    return (value_rows * inverse_rms, inverse_rms)


def norm_back(back_unit, unit_rows, inverse_rms):
    return inverse_rms * (
        back_unit - unit_rows * jnp.mean(back_unit * unit_rows, -1, keepdims=True)
    )


def to_heads(value_rows, sequence_count, token_positions):
    group_total = QUERY_HEADS // KEYVAL_HEADS
    return (
        value_rows.reshape(sequence_count, token_positions, KEYVAL_HEADS, group_total, HEAD_WIDTH)
        .transpose(0, 2, 3, 1, 4)
        .reshape(sequence_count * KEYVAL_HEADS, group_total * token_positions, HEAD_WIDTH)
    )


def from_heads(value_rows, sequence_count, token_positions):
    group_total = QUERY_HEADS // KEYVAL_HEADS
    return (
        value_rows.reshape(sequence_count, KEYVAL_HEADS, group_total, token_positions, HEAD_WIDTH)
        .transpose(0, 3, 1, 2, 4)
        .reshape(sequence_count, token_positions, QUERY_HEADS * HEAD_WIDTH)
    )


def per_sequence(value_rows, sequence_count):
    return value_rows.reshape((sequence_count, KEYVAL_HEADS) + value_rows.shape[1:])


def masked_scores(query_group, key_group, allowed):
    raw_scores = jnp.einsum("qd,kd->qk", query_group, key_group, preferred_element_type=jnp.float32)
    return jnp.where(allowed, raw_scores * HEAD_WIDTH ** (-0.5), -jnp.inf)


def head_forward(head_items, allowed):
    query_group, key_group, value_group = head_items
    scores = masked_scores(query_group, key_group, allowed)
    row_top = jnp.max(scores, -1, keepdims=True)
    lifted = jnp.exp(scores - row_top)
    row_total = jnp.sum(lifted, -1, keepdims=True)
    weights = (lifted / row_total).astype(jnp.bfloat16)
    mixed_heads = jnp.einsum("qk,kd->qd", weights, value_group, preferred_element_type=jnp.float32)
    return (mixed_heads, row_top[:, 0], row_total[:, 0])


def head_backward(head_items, allowed):
    query_group, key_group, value_group, back_mixed, row_top, row_total = head_items
    scores = masked_scores(query_group, key_group, allowed)
    weights = jnp.exp(scores - row_top[:, None]) / row_total[:, None]
    back_weights = jnp.einsum(
        "qd,kd->qk", back_mixed, value_group, preferred_element_type=jnp.float32
    )
    weighted_sum = jnp.sum(weights * back_weights, -1, keepdims=True)
    back_scores = (weights * (back_weights - weighted_sum)).astype(jnp.bfloat16)
    back_query = jnp.einsum(
        "qk,kd->qd", back_scores, key_group, preferred_element_type=jnp.float32
    ) * HEAD_WIDTH ** (-0.5)
    back_key = jnp.einsum(
        "qk,qd->kd", back_scores, query_group, preferred_element_type=jnp.float32
    ) * HEAD_WIDTH ** (-0.5)
    back_value = jnp.einsum(
        "qk,qd->kd", weights.astype(jnp.bfloat16), back_mixed, preferred_element_type=jnp.float32
    )
    return (back_query, back_key, back_value)


def on_device(
    tokens, cotangent, input_gain, w_query, w_keyval, w_output, middle_gain, w_gate, w_up, w_down
):
    sequence_count = tokens.shape[0]
    token_positions = tokens.shape[1]
    group_total = QUERY_HEADS // KEYVAL_HEADS
    place_index = lax.axis_index("ctx") * lax.axis_size("tp") + lax.axis_index("tp")
    first_place = place_index * token_positions
    cosine_table, sine_table = rope_tables(token_positions, first_place)
    query_place = first_place + lax.iota(jnp.int32, group_total * token_positions) % token_positions
    allowed = lax.iota(jnp.int32, SEQUENCE_LENGTH)[None, :] <= query_place[:, None]
    full_gain_one, full_query, full_keyval, full_output = (
        lax.all_gather(input_gain, "fsdp", axis=0, tiled=True),
        lax.all_gather(w_query, "fsdp", axis=0, tiled=True),
        lax.all_gather(w_keyval, "fsdp", axis=0, tiled=True),
        lax.all_gather(w_output, "fsdp", axis=0, tiled=True),
    )
    gain_one = full_gain_one.astype(jnp.float32)
    inputs = tokens.astype(jnp.float32)
    unit_one, inverse_one = normalize(inputs)
    normed_one = (unit_one * gain_one).astype(jnp.bfloat16)
    query_raw = jnp.dot(normed_one, full_query, preferred_element_type=jnp.float32)
    keyval_unrotated = jnp.dot(normed_one, full_keyval, preferred_element_type=jnp.float32)
    query_low = apply_rotary(query_raw, cosine_table, sine_table, QUERY_HEADS).astype(jnp.bfloat16)
    keyval_low = jnp.concatenate(
        [
            apply_rotary(keyval_unrotated[..., :KEY_WIDTH], cosine_table, sine_table, KEYVAL_HEADS),
            keyval_unrotated[..., KEY_WIDTH:],
        ],
        -1,
    ).astype(jnp.bfloat16)
    keyval_gathered = lax.all_gather(keyval_low, ("ctx", "tp"), axis=1, tiled=True)
    query_heads = to_heads(query_low, sequence_count, token_positions)
    stacked = (
        keyval_gathered.reshape(sequence_count, SEQUENCE_LENGTH, 2, KEYVAL_HEADS, HEAD_WIDTH)
        .transpose(2, 0, 3, 1, 4)
        .reshape(2, sequence_count * KEYVAL_HEADS, SEQUENCE_LENGTH, HEAD_WIDTH)
    )
    key_heads = stacked[0]
    value_heads = stacked[1]
    mixed_heads, row_top, row_total = lax.map(
        partial(head_forward, allowed=allowed), (query_heads, key_heads, value_heads)
    )
    mixed_low = from_heads(mixed_heads, sequence_count, token_positions).astype(jnp.bfloat16)
    attention_out = jnp.dot(mixed_low, full_output, preferred_element_type=jnp.float32)
    middle = inputs + attention_out
    full_gate, full_up, full_down, full_gain_two = (
        lax.all_gather(w_gate, "fsdp", axis=0, tiled=True),
        lax.all_gather(w_up, "fsdp", axis=0, tiled=True),
        lax.all_gather(w_down, "fsdp", axis=0, tiled=True),
        lax.all_gather(middle_gain, "fsdp", axis=0, tiled=True),
    )
    gain_two = full_gain_two.astype(jnp.float32)
    unit_two, inverse_two = normalize(middle)
    normed_two = (unit_two * gain_two).astype(jnp.bfloat16)
    pair_rows, pair_cotangent = (
        lax.all_gather(normed_two, "tp", axis=1, tiled=True),
        lax.all_gather(cotangent, "tp", axis=1, tiled=True),
    )
    gate_proj = jnp.dot(pair_rows, full_gate, preferred_element_type=jnp.float32)
    up_proj = jnp.dot(pair_rows, full_up, preferred_element_type=jnp.float32)
    sigmoid_gate = jax.nn.sigmoid(gate_proj)
    swish_gate = gate_proj * sigmoid_gate
    hidden = (swish_gate * up_proj).astype(jnp.bfloat16)
    branch_part = jnp.einsum("spf,df->spd", hidden, full_down, preferred_element_type=jnp.float32)
    feed_out = lax.psum_scatter(
        branch_part.astype(jnp.bfloat16), "tp", scatter_dimension=1, tiled=True
    ).astype(jnp.float32)
    result = (middle + feed_out).astype(jnp.bfloat16)
    back_hidden = jnp.dot(pair_cotangent, full_down, preferred_element_type=jnp.float32)
    back_gate = (
        back_hidden * up_proj * sigmoid_gate * (1.0 + gate_proj * (1.0 - sigmoid_gate))
    ).astype(jnp.bfloat16)
    back_up = (back_hidden * swish_gate).astype(jnp.bfloat16)
    grad_down = jnp.einsum(
        "spd,spf->df", pair_cotangent, hidden, preferred_element_type=jnp.float32
    )
    grad_gate = jnp.einsum("spd,spf->df", pair_rows, back_gate, preferred_element_type=jnp.float32)
    grad_up = jnp.einsum("spd,spf->df", pair_rows, back_up, preferred_element_type=jnp.float32)
    back_normed_part = jnp.einsum(
        "spf,df->spd", back_gate, full_gate, preferred_element_type=jnp.float32
    ) + jnp.einsum("spf,df->spd", back_up, full_up, preferred_element_type=jnp.float32)
    back_normed_two = lax.psum_scatter(back_normed_part, "tp", scatter_dimension=1, tiled=True)
    grad_gain_two = jnp.sum(back_normed_two * unit_two, axis=(0, 1))
    back_middle = cotangent.astype(jnp.float32) + norm_back(
        back_normed_two * gain_two, unit_two, inverse_two
    )
    back_attention = back_middle.astype(jnp.bfloat16)
    grad_output = jnp.einsum(
        "spq,spd->qd", mixed_low, back_attention, preferred_element_type=jnp.float32
    )
    back_mixed = jnp.einsum(
        "spd,qd->spq", back_attention, full_output, preferred_element_type=jnp.float32
    ).astype(jnp.bfloat16)

    def attend_back(carried, sequence_items):
        back_query, back_key, back_value = lax.map(
            partial(head_backward, allowed=allowed), sequence_items
        )
        back_keyval = (
            jnp.stack([back_key, back_value])
            .transpose(2, 0, 1, 3)
            .reshape(SEQUENCE_LENGTH, 2 * KEY_WIDTH)
        )
        owned_rows = lax.psum_scatter(
            back_keyval.astype(jnp.bfloat16), ("ctx", "tp"), scatter_dimension=0, tiled=True
        ).astype(jnp.float32)
        return (carried, (back_query, owned_rows))

    sequence_items = tuple(
        (
            per_sequence(value_rows, sequence_count)
            for value_rows in (
                query_heads,
                key_heads,
                value_heads,
                to_heads(back_mixed, sequence_count, token_positions),
                row_top,
                row_total,
            )
        )
    )
    unused, (query_gradient_full, owned_tokens_full) = lax.scan(
        attend_back, jnp.zeros((), jnp.float32), sequence_items
    )
    back_query_rows = from_heads(
        query_gradient_full.reshape(
            (sequence_count * KEYVAL_HEADS,) + query_gradient_full.shape[2:]
        ),
        sequence_count,
        token_positions,
    )
    back_query_low = apply_rotary(back_query_rows, cosine_table, -sine_table, QUERY_HEADS).astype(
        jnp.bfloat16
    )
    back_keyval_low = jnp.concatenate(
        [
            apply_rotary(
                owned_tokens_full[..., :KEY_WIDTH], cosine_table, -sine_table, KEYVAL_HEADS
            ),
            owned_tokens_full[..., KEY_WIDTH:],
        ],
        -1,
    ).astype(jnp.bfloat16)
    grad_query = jnp.einsum(
        "spd,spq->dq", normed_one, back_query_low, preferred_element_type=jnp.float32
    )
    grad_keyval = jnp.einsum(
        "spd,spk->dk", normed_one, back_keyval_low, preferred_element_type=jnp.float32
    )
    back_normed_one = jnp.einsum(
        "spq,dq->spd", back_query_low, full_query, preferred_element_type=jnp.float32
    ) + jnp.einsum("spk,dk->spd", back_keyval_low, full_keyval, preferred_element_type=jnp.float32)
    grad_gain_one = jnp.sum(back_normed_one * unit_one, axis=(0, 1))
    back_inputs = back_middle + norm_back(back_normed_one * gain_one, unit_one, inverse_one)
    attention_term = jnp.concatenate([grad_query, grad_keyval, grad_output], 1)
    feed_term = jnp.concatenate([grad_gate, grad_up, grad_down], 1)
    attention_total, gain_one_total, gain_two_total = (
        lax.psum(attention_term.astype(jnp.bfloat16), ("ctx", "tp")).astype(jnp.float32),
        lax.psum(grad_gain_one.astype(jnp.bfloat16), ("ctx", "tp")).astype(jnp.float32),
        lax.psum(grad_gain_two.astype(jnp.bfloat16), ("ctx", "tp")).astype(jnp.float32),
    )
    feed_total = lax.psum(feed_term.astype(jnp.bfloat16), "ctx")
    attention_share, feed_share, gain_one_share, gain_two_share = (
        lax.psum_scatter(
            attention_total.astype(jnp.bfloat16), "fsdp", scatter_dimension=0, tiled=True
        ).astype(jnp.float32),
        lax.psum_scatter(feed_total, "fsdp", scatter_dimension=0, tiled=True).astype(jnp.float32),
        lax.psum_scatter(
            gain_one_total.astype(jnp.bfloat16), "fsdp", scatter_dimension=0, tiled=True
        ).astype(jnp.float32),
        lax.psum_scatter(
            gain_two_total.astype(jnp.bfloat16), "fsdp", scatter_dimension=0, tiled=True
        ).astype(jnp.float32),
    )
    query_width = full_query.shape[1]
    keyval_width = full_keyval.shape[1]
    hidden_width = full_gate.shape[1]
    share_query = attention_share[:, :query_width]
    share_keyval = attention_share[:, query_width : query_width + keyval_width]
    share_output = attention_share[:, query_width + keyval_width :]
    share_gate = feed_share[:, :hidden_width]
    share_up = feed_share[:, hidden_width : 2 * hidden_width]
    share_down = feed_share[:, 2 * hidden_width :]
    return (
        result,
        back_inputs,
        gain_one_share,
        share_query,
        share_keyval,
        share_output,
        gain_two_share,
        share_gate,
        share_up,
        share_down,
    )


def solution(mesh):
    in_specs = (
        P("fsdp", ("ctx", "tp"), None),
        P("fsdp", ("ctx", "tp"), None),
        P("fsdp"),
        P("fsdp", None),
        P("fsdp", None),
        P("fsdp", None),
        P("fsdp"),
        P("fsdp", "tp"),
        P("fsdp", "tp"),
        P("fsdp", "tp"),
    )
    out_specs = (
        P("fsdp", ("ctx", "tp"), None),
        P("fsdp", ("ctx", "tp"), None),
        P("fsdp"),
        P("fsdp", None),
        P("fsdp", None),
        P("fsdp", None),
        P("fsdp"),
        P("fsdp", "tp"),
        P("fsdp", "tp"),
        P("fsdp", "tp"),
    )
    return jax.shard_map(
        on_device, mesh=mesh, in_specs=in_specs, out_specs=out_specs, check_vma=False
    )
```

profile of v0, /device:TPU:0, one launch (start us, length us, event | category | flops | bytes accessed | tf_op | source)
XLA Modules:
  0.0 1055.6 jit_solution(356635097389830232)
XLA Ops:
  12.4 8.3 all-reduce.6
  23.0 7.0 all-gather.12.cloned.1.call-done
  37.5 16.0 %all-gather.10.cloned.1.call-done = bf16[960,960]{1,0:T(8,128)(2,1)} async-done(((bf16[240,960]{1,0:T(8,128)(2,1)}), bf16[960,960]{1,0:T(8,128)(2,1)}) %all-gather.10.cloned.1.call-update) | async-done | bytes 1843216 | tf_op jit(solution)/shard_map/all_gather | solution.py:124
  58.6 84.0 %all-gather.14.cloned.1.call-done = bf16[2,2048,640]{2,1,0:T(8,128)(2,1)} async-done(((bf16[2,256,640]{2,1,0:T(8,128)(2,1)}), bf16[2,2048,640]{2,1,0:T(8,128)(2,1)}) %all-gather.14.cloned.1.call-update) | async-done | bytes 5242896 | tf_op jit(solution)/shard_map/all_gather | solution.py:142
  142.6 8.0 copy.72
  150.6 7.3 slice_bitcast_fusion
  157.9 80.6 %while.43 = (s32[]{:T(128)}, bf16[10,768,64]{1,2,0:T(8,128)(2,1)S(1)}, f32[10,768]{1,0:T(8,128)S(1)}, f32[10,768]{1,0:T(8,128)S(1)}, bf16[10,768,64]{2,1,0:T(8,1...) while((s32[]{:T(128)}, ...), condition=%wide.region_4.5_spmd.clone, body=%wide.region_1.4_spmd.clone.sunk | while | flops 426244608 | bytes 19846260 | solution.py:151
  162.3 3.3 fusion.152
  170.4 3.4 fusion.152
  178.5 3.3 fusion.152
  186.5 3.3 fusion.152
  194.5 3.3 fusion.152
  202.6 3.3 fusion.152
  210.7 3.4 fusion.152
  218.8 3.3 fusion.152
  226.8 3.3 fusion.152
  234.9 3.3 fusion.152
  243.4 3.1 multiply_reduce_fusion.3
  248.7 7.6 fusion.58
  256.3 26.9 %all-gather.18.cloned.1.call-done = bf16[2,512,960]{1,2,0:T(8,128)(2,1)} async-done(((bf16[2,256,960]{1,2,0:T(8,128)(2,1)}), bf16[2,512,960]{1,2,0:T(8,128)(2,1)}) %all-gather.18.cloned.1.call-update) | async-done | bytes 1966096 | tf_op jit(solution)/shard_map/all_gather | solution.py:167
  283.1 7.6 fusion.64
  290.7 18.6 %all-gather.20.cloned.1.call-done = bf16[960,1280]{1,0:T(8,128)(2,1)} async-done(((bf16[240,1280]{1,0:T(8,128)(2,1)}), bf16[960,1280]{1,0:T(8,128)(2,1)}) %all-gather.20.cloned.1.call-update) | async-done | bytes 2457616 | tf_op jit(solution)/shard_map/all_gather | solution.py:158
  309.4 11.9 %multiply_convert_fusion.2 = (bf16[2,512,1280]{2,1,0:T(8,128)(2,1)S(1)}, bf16[2,512,1280]{2,1,0:T(8,128)(2,1)S(1)}, bf16[2,512,1280]{2,1,0:T(8,128)(2,1)}) fusion(f32[2,512,1280]{2,1,0:T(8,128)} %fusion.58, f32[2,512,1280]{2,1,0:T(8,128)} %fusion.64, bf16[2,512,960]{1,2,0:T(8,128)(2,1)} %all-gather.18.cloned.1.call-done, ...), kind=kOutput, calls=%fused_computation.71 | convolution fusion | flops 2536243200 | bytes 22773760 | tf_op jit(solution)/shard_map/dot_general | solution.py:170
  324.8 4.9 fusion.85
  329.8 6.5 fusion.88
  336.4 5.6 fusion.53
  342.0 3.4 bitcast_convert_fusion.2
  345.4 3.4 bitcast_convert_fusion.1
  348.9 3.4 pad_maximum_fusion.1
  352.3 29.6 %reduce-scatter.8.cloned.1.call-done = f32[2,256,960]{1,2,0:T(8,128)} async-done(((f32[2,512,960]{1,2,0:T(8,128)}), f32[2,256,960]{1,2,0:T(8,128)}) %reduce-scatter.8.cloned.1.call-update) | async-done | bytes 1966096 | tf_op jit(solution)/shard_map/reduce_scatter | solution.py:193
  384.5 30.1 %reduce-scatter.6.cloned.1.call-done = bf16[2,256,960]{1,2,0:T(8,128)(2,1)} async-done(((bf16[2,512,960]{1,2,0:T(8,128)(2,1)}), bf16[2,256,960]{1,2,0:T(8,128)(2,1)}) %reduce-scatter.6.cloned.1.call-update) | async-done | bytes 983056 | tf_op jit(solution)/shard_map/reduce_scatter | solution.py:176
  414.6 3.5 multiply_add_fusion
  421.2 340.2 %while.45 = (s32[]{:T(128)}, f32[2,5,768,64]{2,3,1,0:T(8,128)}, f32[2,256,640]{1,2,0:T(8,128)}, bf16[2,5,768,64]{3,2,1,0:T(8,128)(2,1)}, bf16[2,5,2048,64]{2,3,1...) while((s32[]{:T(128)}, f32[2,5,768,64]{2,3,1,0:T(8,128)}, ...), condition=%wide.region_14.15_spmd.clone, body=%wide.region_9.14_spmd.clone.sunk | while | flops 1025588480 | bytes 125203080 | solution.py:233
  423.8 3.0 constant_dynamic-slice_fusion.3
  429.5 3.1 copy.95
  435.6 79.8 %while.46 = (s32[]{:T(128)}, f32[5,768,64]{1,2,0:T(8,128)}, bf16[5,2048,64]{1,2,0:T(8,128)(2,1)}, bf16[5,2048,64]{1,2,0:T(8,128)(2,1)}, bf16[5,768,64]{2,1,0:T(8...) while((s32[]{:T(128)}, f32[5,768,64]{1,2,0:T(8,128)}, ...), condition=%wide.region_12.12_spmd, body=%wide.region_10.11_spmd.sunk | while | flops 1022541056 | bytes 79656208 | solution.py:207
  439.1 3.7 multiply_reduce_fusion.5
  455.1 3.7 multiply_reduce_fusion.5
  471.1 3.7 multiply_reduce_fusion.5
  487.0 3.7 multiply_reduce_fusion.5
  503.0 3.7 multiply_reduce_fusion.5
  515.4 3.5 pad_maximum_fusion.11
  521.2 68.9 %reduce-scatter.14.cloned.1.call-done = bf16[256,640]{0,1:T(8,128)(2,1)} async-done(((bf16[2048,640]{0,1:T(8,128)(2,1)}), bf16[256,640]{0,1:T(8,128)(2,1)}) %reduce-scatter.14.cloned.1.call-update) | async-done | bytes 327696 | tf_op jit(solution)/shard_map/while/body/eval_jaxpr/reduce_scatter | solution.py:215
  594.4 3.0 constant_dynamic-slice_fusion.3
  600.1 3.1 copy.95
  606.1 79.8 %while.46 = (s32[]{:T(128)}, f32[5,768,64]{1,2,0:T(8,128)}, bf16[5,2048,64]{1,2,0:T(8,128)(2,1)}, bf16[5,2048,64]{1,2,0:T(8,128)(2,1)}, bf16[5,768,64]{2,1,0:T(8...) while((s32[]{:T(128)}, f32[5,768,64]{1,2,0:T(8,128)}, ...), condition=%wide.region_12.12_spmd, body=%wide.region_10.11_spmd.sunk | while | flops 1022541056 | bytes 79656208 | solution.py:207
  609.7 3.7 multiply_reduce_fusion.5
  625.6 3.7 multiply_reduce_fusion.5
  641.6 3.7 multiply_reduce_fusion.5
  657.6 3.7 multiply_reduce_fusion.5
  673.5 3.7 multiply_reduce_fusion.5
  686.0 3.5 pad_maximum_fusion.11
  691.8 67.5 %reduce-scatter.14.cloned.1.call-done = bf16[256,640]{0,1:T(8,128)(2,1)} async-done(((bf16[2048,640]{0,1:T(8,128)(2,1)}), bf16[256,640]{0,1:T(8,128)(2,1)}) %reduce-scatter.14.cloned.1.call-update) | async-done | bytes 327696 | tf_op jit(solution)/shard_map/while/body/eval_jaxpr/reduce_scatter | solution.py:215
  763.8 3.1 reshape_reshape.14
  779.7 9.3 concatenate.38
  789.1 40.0 %reduce-scatter.12.cloned.1.call-done = bf16[240,3840]{1,0:T(8,128)(2,1)} async-done(((bf16[960,3840]{1,0:T(8,128)(2,1)}), bf16[240,3840]{1,0:T(8,128)(2,1)}) %reduce-scatter.12.cloned.1.call-update) | async-done | bytes 1843216 | tf_op jit(solution)/shard_map/reduce_scatter | solution.py:278
  829.9 3.1 fusion.81
  835.5 5.7 all-reduce.5
  841.4 21.5 %all-reduce.4 = (bf16[240]{0:T(256)(128)(2,1)S(1)}, bf16[240]{0:T(256)(128)(2,1)S(1)}) all-reduce(bf16[240]{0:T(256)(128)(2,1)S(1)} %dynamic-slice.3, bf16[240]{0:T(256)(128)(2,1)S(1)} %dynamic-slice.5), channel_id=1, replica_groups=mesh['fsdp'=4,'ctx'=4,'tp'=2] {'ctx','tp'}, use_global_device_ids=true, to_apply=%region_17.18 | all-reduce | flops 480 | bytes 1920 | tf_op jit(solution)/shard_map/psum | solution.py:270
  864.1 16.8 %reduce-scatter.10.cloned.1.call-done = bf16[240,2560]{1,0:T(8,128)(2,1)} async-done(((bf16[960,2560]{1,0:T(8,128)(2,1)}), bf16[240,2560]{1,0:T(8,128)(2,1)}) %reduce-scatter.10.cloned.1.call-update) | async-done | bytes 1228816 | tf_op jit(solution)/shard_map/reduce_scatter | solution.py:275
  881.0 3.3 fusion.74
  884.3 77.4 %all-reduce.12.cloned.1.call-done = bf16[240,3840]{1,0:T(8,128)(2,1)} async-done(((bf16[240,3840]{1,0:T(8,128)(2,1)}), bf16[240,3840]{1,0:T(8,128)(2,1)}) %all-reduce.12.cloned.1.call-update) | async-done | bytes 1843216 | tf_op jit(solution)/shard_map/psum | solution.py:273
  961.7 3.4 fusion.112
  965.0 80.2 %all-reduce.10.cloned.1.call-done = bf16[240,2560]{1,0:T(8,128)(2,1)} async-done(((bf16[240,2560]{1,0:T(8,128)(2,1)}), bf16[240,2560]{1,0:T(8,128)(2,1)}) %all-reduce.10.cloned.1.call-update) | async-done | bytes 1228816 | tf_op jit(solution)/shard_map/psum | solution.py:269
  (417 shorter events, 251.3 us)
Async XLA Ops:
  7.2 22.9 %copy-start.11 = (bf16[2,256,960]{1,2,0:T(8,128)(2,1)S(1)}, bf16[2,256,960]{1,2,0:T(8,128)(2,1)}, u32[]{:S(2)}) copy-start(bf16[2,256,960]{1,2,0:T(8,128)(2,1)} %param.16) | copy-start | bytes 2949124
  7.2 22.9 %all-gather.12.cloned.1.call-start = ((), (), s32[]{:S(2)}) async-start(), calls=%async_computation.6 | async-start | bytes 1536000 | tf_op jit(solution)/shard_map/all_gather | solution.py:125
  7.9 45.6 %all-gather.10.cloned.1.call-start = ((), (), s32[]{:S(2)}) async-start(), calls=%async_computation.5 | async-start | bytes 2457600 | tf_op jit(solution)/shard_map/all_gather | solution.py:124
  8.7 133.9 %all-gather.14.cloned.1.call-start = ((), (), s32[]{:S(2)}) async-start(), calls=%async_computation.7 | async-start | bytes 5898240 | tf_op jit(solution)/shard_map/all_gather | solution.py:142
  20.8 32.8 %copy-start.28 = (f32[960]{0:T(1024)}, f32[960]{0:T(1024)S(1)}, u32[]{:S(2)}) copy-start(f32[960]{0:T(1024)S(1)} %convert_element_type.123) | copy-start | bytes 11524
  22.2 31.3 %copy-start.31 = (f32[2,256]{1,0:T(2,128)}, f32[2,256]{1,0:T(2,128)S(1)}, u32[]{:S(2)}) copy-start(f32[2,256]{1,0:T(2,128)S(1)} %add_rsqrt_fusion.1) | copy-start | bytes 6148
  23.0 33.4 %copy-start.21 = (f32[256,32]{0,1:T(8,128)}, f32[256,32]{0,1:T(8,128)S(1)}, u32[]{:S(2)}) copy-start(f32[256,32]{0,1:T(8,128)S(1)} %get-tuple-element.374) | copy-start | bytes 98308
  34.4 208.9 %all-gather.16.cloned.1.call-start = ((), (), s32[]{:S(2)}) async-start(), calls=%async_computation.8 | async-start | bytes 2457600 | tf_op jit(solution)/shard_map/all_gather | solution.py:126
  35.0 213.7 %all-gather.26.cloned.1.call-start = ((), (), s32[]{:S(2)}) async-start(), calls=%async_computation.14 | async-start | bytes 2949120 | tf_op jit(solution)/shard_map/all_gather | solution.py:168
  35.6 213.1 %all-gather.24.cloned.1.call-start = ((), (), s32[]{:S(2)}) async-start(), calls=%async_computation.12 | async-start | bytes 3072000 | tf_op jit(solution)/shard_map/all_gather | solution.py:160
  36.2 220.1 %all-gather.22.cloned.1.call-start = ((), (), s32[]{:S(2)}) async-start(), calls=%async_computation.11 | async-start | bytes 3072000 | tf_op jit(solution)/shard_map/all_gather | solution.py:159
  36.9 246.2 %all-gather.18.cloned.1.call-start = ((), (), s32[]{:S(2)}) async-start(), calls=%async_computation.9 | async-start | bytes 2949120 | tf_op jit(solution)/shard_map/all_gather | solution.py:167
  150.6 7.3 copy-start.18
  247.7 61.7 %all-gather.20.cloned.1.call-start = ((), (), s32[]{:S(2)}) async-start(), calls=%async_computation.10 | async-start | bytes 3072000 | tf_op jit(solution)/shard_map/all_gather | solution.py:158
  248.5 133.4 %reduce-scatter.8.cloned.1.call-start = ((), (), s32[]{:S(2)}) async-start(), calls=%async_computation.15 | async-start | bytes 5898240 | tf_op jit(solution)/shard_map/reduce_scatter | solution.py:193
  309.4 11.9 %copy-start.33 = (bf16[960,1280]{1,0:T(8,128)(2,1)S(1)}, bf16[960,1280]{1,0:T(8,128)(2,1)}, u32[]{:S(2)}) copy-start(bf16[960,1280]{1,0:T(8,128)(2,1)} %all-gather.22.cloned.1.call-done) | copy-start | bytes 7372804
  321.3 2.8 copy-start.38
  321.3 2.8 copy-start.40
  321.3 3.5 copy-start.34
  329.7 84.9 %reduce-scatter.6.cloned.1.call-start = ((), (), s32[]{:S(2)}) async-start(), calls=%async_computation.13 | async-start | bytes 2949120 | tf_op jit(solution)/shard_map/reduce_scatter | solution.py:176
  336.4 5.6 copy-start.36
  336.4 5.6 copy-start.41
  342.0 3.5 copy-start.39
  352.2 62.4 %copy-start.10 = (bf16[2,256,960]{1,2,0:T(8,128)(2,1)S(1)}, bf16[2,256,960]{1,2,0:T(8,128)(2,1)}, u32[]{:S(2)}) copy-start(bf16[2,256,960]{1,2,0:T(8,128)(2,1)} %param.17) | copy-start | bytes 2949124
  414.6 3.5 copy-start.35
  421.6 168.5 %reduce-scatter.14.cloned.1.call-start = ((), (), s32[]{:S(2)}) async-start(), calls=%async_computation.20 | async-start | bytes 2949120 | tf_op jit(solution)/shard_map/while/body/eval_jaxpr/reduce_scatter | solution.py:215
  445.8 2.9 copy-start.3
  448.7 2.8 copy-start.1
  461.7 2.9 copy-start.3
  464.7 2.8 copy-start.1
  477.7 2.9 copy-start.3
  480.6 2.8 copy-start.1
  493.7 2.9 copy-start.3
  496.6 2.9 copy-start.1
  509.7 2.9 copy-start.3
  512.6 2.8 copy-start.1
  519.0 71.1 %copy-start.13 = (f32[2,256,640]{1,2,0:T(8,128)S(1)}, f32[2,256,640]{1,2,0:T(8,128)}, u32[]{:S(2)}) copy-start(f32[2,256,640]{1,2,0:T(8,128)} %get-tuple-element.691) | copy-start | bytes 3932164 | tf_op jit(solution)/shard_map/while
  592.2 167.1 %reduce-scatter.14.cloned.1.call-start = ((), (), s32[]{:S(2)}) async-start(), calls=%async_computation.20 | async-start | bytes 2949120 | tf_op jit(solution)/shard_map/while/body/eval_jaxpr/reduce_scatter | solution.py:215
  616.3 2.9 copy-start.3
  619.3 2.9 copy-start.1
  632.3 2.9 copy-start.3
  635.2 2.8 copy-start.1
  648.2 2.9 copy-start.3
  651.2 2.8 copy-start.1
  664.2 2.9 copy-start.3
  667.1 2.9 copy-start.1
  680.2 2.9 copy-start.3
  683.1 2.8 copy-start.1
  689.5 69.8 %copy-start.13 = (f32[2,256,640]{1,2,0:T(8,128)S(1)}, f32[2,256,640]{1,2,0:T(8,128)}, u32[]{:S(2)}) copy-start(f32[2,256,640]{1,2,0:T(8,128)} %get-tuple-element.691) | copy-start | bytes 3932164 | tf_op jit(solution)/shard_map/while
  761.4 67.7 %reduce-scatter.12.cloned.1.call-start = ((), (), s32[]{:S(2)}) async-start(), calls=%async_computation.18 | async-start | bytes 9216000 | tf_op jit(solution)/shard_map/reduce_scatter | solution.py:278
  761.9 119.0 %reduce-scatter.10.cloned.1.call-start = ((), (), s32[]{:S(2)}) async-start(), calls=%async_computation.16 | async-start | bytes 6144000 | tf_op jit(solution)/shard_map/reduce_scatter | solution.py:275
  766.9 2.6 copy-start.22
  766.9 2.6 copy-start.27
  768.6 2.2 copy-start.8
  772.6 2.1 copy-start.20
  774.7 2.5 copy-start.7
  774.7 2.5 copy-start.17
  789.0 172.6 %all-reduce.12.cloned.1.call-start = ((), (), s32[]{:S(2)}) async-start(), calls=%async_computation.19 | async-start | bytes 3686400 | tf_op jit(solution)/shard_map/psum | solution.py:273
  829.1 216.1 %all-reduce.10.cloned.1.call-start = ((), (), s32[]{:S(2)}) async-start(), calls=%async_computation.17 | async-start | bytes 2457600 | tf_op jit(solution)/shard_map/psum | solution.py:269
  829.8 3.2 copy-start.24
  829.8 3.1 copy-start.26
  829.8 3.1 copy-start.37
  833.0 2.5 copy-start.30
  1045.3 2.1 copy-start.9
  (43 other events, 64.0 us)
Sparse Core Ops, SparseCore 0:
  9.6 20.4 all-gather.11
  31.6 21.8 all-gather.9
  56.3 86.2 all-gather.13
  144.0 20.0 all-gather.15
  165.4 31.5 all-gather.25
  198.5 24.6 all-gather.23
  224.8 24.5 all-gather.21
  251.5 31.5 all-gather.17
  284.7 24.6 all-gather.19
  329.8 51.9 reduce-scatter.7
  384.2 30.3 reduce-scatter.5
  519.1 70.9 reduce-scatter.13
  689.7 69.5 reduce-scatter.13
  764.4 64.6 reduce-scatter.11
  831.7 49.1 reduce-scatter.9
  883.2 78.4 all-reduce.11
  965.0 80.1 all-reduce.9
where the time goes:
time: 1060 us
  waiting for transfers between devices  568 us (54%)
  matrix products  260 us (25%)
  local copies, waits for them, and re-layouts  112 us (11%)
  other arithmetic  60.4 us (6%)
  blocking collectives  35.6 us (3%)
  between operations  16 us (2%)
    reduce_scatter x2, waiting for transfers between devices, attend_back(): lax.psum_scatter(back_keyval.astype(jnp.bfloat16), ('ctx', 'tp'), scatter...  136 us
    all_gather x1, waiting for transfers between devices, on_device(): lax.all_gather(keyval_low, ('ctx', 'tp'), axis=1, tiled=True)  84 us
    psum x1, waiting for transfers between devices, on_device(): lax.psum(attention_term.astype(jnp.bfloat16), ('ctx', 'tp'))  80.2 us
    psum x1, waiting for transfers between devices, on_device(): feed_total = lax.psum(feed_term.astype(jnp.bfloat16), 'ctx')  77.4 us
    dot_general x20, matrix products, masked_scores(): jnp.einsum('qd,kd->qk', query_group, key_group, preferred_element_type=jn...  60.3 us
    reduce_scatter x1, waiting for transfers between devices, on_device(): lax.psum_scatter(feed_total, 'fsdp', scatter_dimension=0, tiled=True)  40 us
    dot_general x10, matrix products, head_forward(): jnp.einsum('qk,kd->qd', weights, value_group, preferred_element_type=jnp....  33.4 us
    reduce_scatter x1, waiting for transfers between devices, on_device(): lax.psum_scatter(branch_part.astype(jnp.bfloat16), 'tp', scatter_dimensio...  30.1 us
  transfers between devices with their start and end apart: 17, of which 13 were waited for; matrix products, arithmetic and copies ran while one was open for 19% of the time, Pallas kernels for 0%

commit v1 on v0

--- a/solution.py
+++ b/solution.py
@@ -1,8 +1,10 @@
+import functools
 from functools import partial
 import jax
 import jax.numpy as jnp
 from jax import lax
 from jax.sharding import PartitionSpec as P
+from jax.lax import psum
 
 QUERY_HEADS = 15
 KEYVAL_HEADS = 5
@@ -11,6 +13,15 @@
 KEY_WIDTH = 320
 EPS = 1e-05
 THETA = 10000.0
+
+
+def end_the_islands(local, axis_name, net_axis):
+    for to_i in (axis_name, net_axis):
+        local = psum(local, to_i)
+    return local
+
+
+_settle_stages_all = functools.partial(end_the_islands, axis_name="tp", net_axis="ctx")
 
 
 def rope_tables(token_positions, first_place):
@@ -266,7 +277,7 @@
     attention_term = jnp.concatenate([grad_query, grad_keyval, grad_output], 1)
     feed_term = jnp.concatenate([grad_gate, grad_up, grad_down], 1)
     attention_total, gain_one_total, gain_two_total = (
-        lax.psum(attention_term.astype(jnp.bfloat16), ("ctx", "tp")).astype(jnp.float32),
+        _settle_stages_all(attention_term.astype(jnp.bfloat16)).astype(jnp.float32),
         lax.psum(grad_gain_one.astype(jnp.bfloat16), ("ctx", "tp")).astype(jnp.float32),
         lax.psum(grad_gain_two.astype(jnp.bfloat16), ("ctx", "tp")).astype(jnp.float32),
     )

time: 1060 us -> 1090 us (1.028)
  waiting for transfers between devices: 568 us -> 598 us
    psum x2, waiting for transfers between devices: 158 us -> 129 us  [end_the_islands(): local = psum(local, to_i)]
    reduce_scatter x1, waiting for transfers between devices: 40 us -> 68.2 us  [on_device(): lax.psum_scatter(feed_total, 'fsdp', scatter_dimension=0, tiled=True)]
    reduce_scatter x1, waiting for transfers between devices: 29.6 us -> 45.5 us  [on_device(): lax.psum_scatter(back_normed_part, 'tp', scatter_dimension=1, tiled=True)]
    reduce_scatter x1, waiting for transfers between devices: 16.8 us -> 31.6 us  [on_device(): lax.psum_scatter(attention_total.astype(jnp.bfloat16), 'fsdp', scatter_di...]
  transfers between devices with their start and end apart: 17 -> 17, of which waited for: 13 -> 13; matrix products, arithmetic and copies ran while one was open for 19% -> 16% of each run, Pallas kernels for 0% -> 0%
where the time goes in v1:
time: 1090 us
  waiting for transfers between devices  598 us (55%)
  matrix products  261 us (24%)
  local copies, waits for them, and re-layouts  113 us (10%)
  other arithmetic  60.1 us (6%)
  blocking collectives  36.7 us (3%)
  between operations  16 us (1%)
    reduce_scatter x2, waiting for transfers between devices, attend_back(): lax.psum_scatter(back_keyval.astype(jnp.bfloat16), ('ctx', 'tp'), scatter...  137 us
    psum x2, waiting for transfers between devices, end_the_islands(): local = psum(local, to_i)  129 us
    all_gather x1, waiting for transfers between devices, on_device(): lax.all_gather(keyval_low, ('ctx', 'tp'), axis=1, tiled=True)  84 us
    reduce_scatter x1, waiting for transfers between devices, on_device(): lax.psum_scatter(feed_total, 'fsdp', scatter_dimension=0, tiled=True)  68.2 us
    dot_general x20, matrix products, masked_scores(): jnp.einsum('qd,kd->qk', query_group, key_group, preferred_element_type=jn...  60.2 us
    reduce_scatter x1, waiting for transfers between devices, on_device(): lax.psum_scatter(back_normed_part, 'tp', scatter_dimension=1, tiled=True)  45.5 us
    dot_general x10, matrix products, head_forward(): jnp.einsum('qk,kd->qd', weights, value_group, preferred_element_type=jnp....  33.4 us
    reduce_scatter x1, waiting for transfers between devices, on_device(): lax.psum_scatter(attention_total.astype(jnp.bfloat16), 'fsdp', scatter_di...  31.6 us
  transfers between devices with their start and end apart: 17, of which 13 were waited for; matrix products, arithmetic and copies ran while one was open for 16% of the time, Pallas kernels for 0%

profile of v1, /device:TPU:0, one launch (start us, length us, event | category | flops | bytes accessed | tf_op | source)
XLA Modules:
  0.0 1086.8 jit_solution(14684172461169726925)
XLA Ops:
  12.4 8.3 all-reduce.7
  23.0 7.0 all-gather.12.cloned.1.call-done
  37.2 16.3 %all-gather.10.cloned.1.call-done = bf16[960,960]{1,0:T(8,128)(2,1)} async-done(((bf16[240,960]{1,0:T(8,128)(2,1)}), bf16[960,960]{1,0:T(8,128)(2,1)}) %all-gather.10.cloned.1.call-update) | async-done | bytes 1843216 | tf_op jit(solution)/shard_map/all_gather | solution.py:135
  58.6 84.0 %all-gather.14.cloned.1.call-done = bf16[2,2048,640]{2,1,0:T(8,128)(2,1)} async-done(((bf16[2,256,640]{2,1,0:T(8,128)(2,1)}), bf16[2,2048,640]{2,1,0:T(8,128)(2,1)}) %all-gather.14.cloned.1.call-update) | async-done | bytes 5242896 | tf_op jit(solution)/shard_map/all_gather | solution.py:153
  142.6 8.0 copy.72
  150.6 7.4 slice_bitcast_fusion
  158.0 80.5 %while.43 = (s32[]{:T(128)}, bf16[10,768,64]{1,2,0:T(8,128)(2,1)S(1)}, f32[10,768]{1,0:T(8,128)S(1)}, f32[10,768]{1,0:T(8,128)S(1)}, bf16[10,768,64]{2,1,0:T(8,1...) while((s32[]{:T(128)}, ...), condition=%wide.region_4.5_spmd.clone, body=%wide.region_1.4_spmd.clone.sunk | while | flops 426244608 | bytes 19846260 | solution.py:162
  162.5 3.3 fusion.152
  170.5 3.4 fusion.152
  178.6 3.3 fusion.152
  186.6 3.3 fusion.152
  194.6 3.3 fusion.152
  202.7 3.3 fusion.152
  210.8 3.3 fusion.152
  218.8 3.3 fusion.152
  226.9 3.3 fusion.152
  234.9 3.3 fusion.152
  243.4 3.1 multiply_reduce_fusion.3
  249.0 7.6 fusion.58
  256.6 26.6 %all-gather.18.cloned.1.call-done = bf16[2,512,960]{1,2,0:T(8,128)(2,1)} async-done(((bf16[2,256,960]{1,2,0:T(8,128)(2,1)}), bf16[2,512,960]{1,2,0:T(8,128)(2,1)}) %all-gather.18.cloned.1.call-update) | async-done | bytes 1966096 | tf_op jit(solution)/shard_map/all_gather | solution.py:178
  283.1 7.6 fusion.64
  290.8 18.6 %all-gather.20.cloned.1.call-done = bf16[960,1280]{1,0:T(8,128)(2,1)} async-done(((bf16[240,1280]{1,0:T(8,128)(2,1)}), bf16[960,1280]{1,0:T(8,128)(2,1)}) %all-gather.20.cloned.1.call-update) | async-done | bytes 2457616 | tf_op jit(solution)/shard_map/all_gather | solution.py:169
  309.4 12.0 %multiply_convert_fusion.2 = (bf16[2,512,1280]{2,1,0:T(8,128)(2,1)S(1)}, bf16[2,512,1280]{2,1,0:T(8,128)(2,1)S(1)}, bf16[2,512,1280]{2,1,0:T(8,128)(2,1)}) fusion(f32[2,512,1280]{2,1,0:T(8,128)} %fusion.58, f32[2,512,1280]{2,1,0:T(8,128)} %fusion.64, bf16[2,512,960]{1,2,0:T(8,128)(2,1)} %all-gather.18.cloned.1.call-done, ...), kind=kOutput, calls=%fused_computation.71 | convolution fusion | flops 2536243200 | bytes 22773760 | tf_op jit(solution)/shard_map/dot_general | solution.py:181
  324.9 4.9 fusion.85
  329.8 6.5 fusion.88
  336.4 45.5 %reduce-scatter.8.cloned.1.call-done = f32[2,256,960]{1,2,0:T(8,128)} async-done(((f32[2,512,960]{1,2,0:T(8,128)}), f32[2,256,960]{1,2,0:T(8,128)}) %reduce-scatter.8.cloned.1.call-update) | async-done | bytes 1966096 | tf_op jit(solution)/shard_map/reduce_scatter | solution.py:204
  384.6 30.0 %reduce-scatter.6.cloned.1.call-done = bf16[2,256,960]{1,2,0:T(8,128)(2,1)} async-done(((bf16[2,512,960]{1,2,0:T(8,128)(2,1)}), bf16[2,256,960]{1,2,0:T(8,128)(2,1)}) %reduce-scatter.6.cloned.1.call-update) | async-done | bytes 983056 | tf_op jit(solution)/shard_map/reduce_scatter | solution.py:187
  414.7 3.5 multiply_add_fusion
  421.2 340.5 %while.45 = (s32[]{:T(128)}, f32[2,5,768,64]{2,3,1,0:T(8,128)}, f32[2,256,640]{1,2,0:T(8,128)}, bf16[2,5,768,64]{3,2,1,0:T(8,128)(2,1)}, bf16[2,5,2048,64]{2,3,1...) while((s32[]{:T(128)}, f32[2,5,768,64]{2,3,1,0:T(8,128)}, ...), condition=%wide.region_14.15_spmd.clone, body=%wide.region_9.14_spmd.clone.sunk | while | flops 1025588480 | bytes 125203080 | solution.py:244
  423.3 3.0 constant_dynamic-slice_fusion.3
  428.9 3.1 copy.95
  432.1 2.9 dynamic-slice_bitcast_fusion.6
  435.0 80.2 %while.46 = (s32[]{:T(128)}, f32[5,768,64]{1,2,0:T(8,128)}, bf16[5,2048,64]{1,2,0:T(8,128)(2,1)}, bf16[5,2048,64]{1,2,0:T(8,128)(2,1)}, bf16[5,768,64]{2,1,0:T(8...) while((s32[]{:T(128)}, f32[5,768,64]{1,2,0:T(8,128)}, ...), condition=%wide.region_12.12_spmd, body=%wide.region_10.11_spmd.sunk | while | flops 1022541056 | bytes 79656208 | solution.py:218
  438.6 3.7 multiply_reduce_fusion.5
  454.7 3.7 multiply_reduce_fusion.5
  470.7 3.7 multiply_reduce_fusion.5
  486.7 3.7 multiply_reduce_fusion.5
  502.8 3.7 multiply_reduce_fusion.5
  515.3 3.4 pad_maximum_fusion.11
  520.9 68.9 %reduce-scatter.14.cloned.1.call-done = bf16[256,640]{0,1:T(8,128)(2,1)} async-done(((bf16[2048,640]{0,1:T(8,128)(2,1)}), bf16[256,640]{0,1:T(8,128)(2,1)}) %reduce-scatter.14.cloned.1.call-update) | async-done | bytes 327696 | tf_op jit(solution)/shard_map/while/body/eval_jaxpr/reduce_scatter | solution.py:226
  594.1 3.0 constant_dynamic-slice_fusion.3
  599.8 3.1 copy.95
  605.9 80.3 %while.46 = (s32[]{:T(128)}, f32[5,768,64]{1,2,0:T(8,128)}, bf16[5,2048,64]{1,2,0:T(8,128)(2,1)}, bf16[5,2048,64]{1,2,0:T(8,128)(2,1)}, bf16[5,768,64]{2,1,0:T(8...) while((s32[]{:T(128)}, f32[5,768,64]{1,2,0:T(8,128)}, ...), condition=%wide.region_12.12_spmd, body=%wide.region_10.11_spmd.sunk | while | flops 1022541056 | bytes 79656208 | solution.py:218
  609.5 3.7 multiply_reduce_fusion.5
  625.5 3.7 multiply_reduce_fusion.5
  641.6 3.7 multiply_reduce_fusion.5
  657.6 3.7 multiply_reduce_fusion.5
  673.7 3.7 multiply_reduce_fusion.5
  686.1 3.4 pad_maximum_fusion.11
  691.8 67.7 %reduce-scatter.14.cloned.1.call-done = bf16[256,640]{0,1:T(8,128)(2,1)} async-done(((bf16[2048,640]{0,1:T(8,128)(2,1)}), bf16[256,640]{0,1:T(8,128)(2,1)}) %reduce-scatter.14.cloned.1.call-update) | async-done | bytes 327696 | tf_op jit(solution)/shard_map/while/body/eval_jaxpr/reduce_scatter | solution.py:226
  765.4 3.7 bitcast_convert_fusion.3
  769.1 3.1 reshape_reshape.14
  780.6 8.6 concatenate.38
  790.8 4.8 fusion.53
  795.6 3.4 bitcast_convert_fusion.2
  799.1 3.4 bitcast_convert_fusion.1
  802.5 3.4 pad_maximum_fusion.1
  806.0 31.6 %reduce-scatter.12.cloned.1.call-done = bf16[240,2560]{1,0:T(8,128)(2,1)} async-done(((bf16[960,2560]{1,0:T(8,128)(2,1)}), bf16[240,2560]{1,0:T(8,128)(2,1)}) %reduce-scatter.12.cloned.1.call-update) | async-done | bytes 1228816 | tf_op jit(solution)/shard_map/reduce_scatter | solution.py:286
  837.6 68.2 %reduce-scatter.10.cloned.1.call-done = bf16[240,3840]{1,0:T(8,128)(2,1)} async-done(((bf16[960,3840]{1,0:T(8,128)(2,1)}), bf16[240,3840]{1,0:T(8,128)(2,1)}) %reduce-scatter.10.cloned.1.call-update) | async-done | bytes 1843216 | tf_op jit(solution)/shard_map/reduce_scatter | solution.py:289
  905.8 46.1 %all-reduce.11.cloned.1.call-done = bf16[240,2560]{1,0:T(8,128)(2,1)} async-done(((bf16[240,2560]{1,0:T(8,128)(2,1)}), bf16[240,2560]{1,0:T(8,128)(2,1)}) %all-reduce.11.cloned.1.call-update) | async-done | bytes 1228816 | tf_op jit(solution)/shard_map/psum | solution.py:20
  958.1 7.0 all-reduce.6
  965.3 21.4 %all-reduce.4 = (bf16[240]{0:T(256)(128)(2,1)S(1)}, bf16[240]{0:T(256)(128)(2,1)S(1)}) all-reduce(bf16[240]{0:T(256)(128)(2,1)S(1)} %dynamic-slice.3, bf16[240]{0:T(256)(128)(2,1)S(1)} %dynamic-slice.5), channel_id=1, replica_groups=mesh['fsdp'=4,'ctx'=4,'tp'=2] {'ctx','tp'}, use_global_device_ids=true, to_apply=%region_17.18 | all-reduce | flops 480 | bytes 1920 | tf_op jit(solution)/shard_map/psum | solution.py:281
  987.8 3.3 fusion.74
  991.1 82.8 %all-reduce.13.cloned.1.call-done = (bf16[240,2560]{1,0:T(8,128)(2,1)}, bf16[240,3840]{1,0:T(8,128)(2,1)}) async-done(((bf16[240,2560]{1,0:T(8,128)(2,1)}, bf16[240,3840]{1,0:T(8,128)(2,1)}), (bf16[240,2560]{1,0:T(8,128)(2,1)}, bf16[240,3840]{1,0:T(8,128)(2,1)})) %all-reduce.13.cloned.1.call-update) | async-done | bytes 3072016 | tf_op jit(solution)/shard_map/psum | solution.py:20
  (419 shorter events, 252.9 us)
Async XLA Ops:
  7.2 22.9 %copy-start.12 = (bf16[2,256,960]{1,2,0:T(8,128)(2,1)S(1)}, bf16[2,256,960]{1,2,0:T(8,128)(2,1)}, u32[]{:S(2)}) copy-start(bf16[2,256,960]{1,2,0:T(8,128)(2,1)} %param.16) | copy-start | bytes 2949124
  7.2 22.9 %all-gather.12.cloned.1.call-start = ((), (), s32[]{:S(2)}) async-start(), calls=%async_computation.6 | async-start | bytes 1536000 | tf_op jit(solution)/shard_map/all_gather | solution.py:136
  7.9 45.6 %all-gather.10.cloned.1.call-start = ((), (), s32[]{:S(2)}) async-start(), calls=%async_computation.5 | async-start | bytes 2457600 | tf_op jit(solution)/shard_map/all_gather | solution.py:135
  8.7 133.9 %all-gather.14.cloned.1.call-start = ((), (), s32[]{:S(2)}) async-start(), calls=%async_computation.7 | async-start | bytes 5898240 | tf_op jit(solution)/shard_map/all_gather | solution.py:153
  20.8 32.8 %copy-start.28 = (f32[960]{0:T(1024)}, f32[960]{0:T(1024)S(1)}, u32[]{:S(2)}) copy-start(f32[960]{0:T(1024)S(1)} %convert_element_type.123) | copy-start | bytes 11524
  22.2 31.3 %copy-start.31 = (f32[2,256]{1,0:T(2,128)}, f32[2,256]{1,0:T(2,128)S(1)}, u32[]{:S(2)}) copy-start(f32[2,256]{1,0:T(2,128)S(1)} %add_rsqrt_fusion.1) | copy-start | bytes 6148
  23.0 33.4 %copy-start.22 = (f32[256,32]{0,1:T(8,128)}, f32[256,32]{0,1:T(8,128)S(1)}, u32[]{:S(2)}) copy-start(f32[256,32]{0,1:T(8,128)S(1)} %get-tuple-element.376) | copy-start | bytes 98308
  34.4 209.0 %all-gather.16.cloned.1.call-start = ((), (), s32[]{:S(2)}) async-start(), calls=%async_computation.8 | async-start | bytes 2457600 | tf_op jit(solution)/shard_map/all_gather | solution.py:137
  35.0 214.0 %all-gather.26.cloned.1.call-start = ((), (), s32[]{:S(2)}) async-start(), calls=%async_computation.14 | async-start | bytes 2949120 | tf_op jit(solution)/shard_map/all_gather | solution.py:179
  35.6 213.4 %all-gather.24.cloned.1.call-start = ((), (), s32[]{:S(2)}) async-start(), calls=%async_computation.12 | async-start | bytes 3072000 | tf_op jit(solution)/shard_map/all_gather | solution.py:171
  36.2 220.4 %all-gather.22.cloned.1.call-start = ((), (), s32[]{:S(2)}) async-start(), calls=%async_computation.11 | async-start | bytes 3072000 | tf_op jit(solution)/shard_map/all_gather | solution.py:170
  36.9 246.2 %all-gather.18.cloned.1.call-start = ((), (), s32[]{:S(2)}) async-start(), calls=%async_computation.9 | async-start | bytes 2949120 | tf_op jit(solution)/shard_map/all_gather | solution.py:178
  150.6 7.4 copy-start.20
  247.8 61.6 %all-gather.20.cloned.1.call-start = ((), (), s32[]{:S(2)}) async-start(), calls=%async_computation.10 | async-start | bytes 3072000 | tf_op jit(solution)/shard_map/all_gather | solution.py:169
  248.5 133.4 %reduce-scatter.8.cloned.1.call-start = ((), (), s32[]{:S(2)}) async-start(), calls=%async_computation.15 | async-start | bytes 5898240 | tf_op jit(solution)/shard_map/reduce_scatter | solution.py:204
  309.4 12.0 %copy-start.33 = (bf16[960,1280]{1,0:T(8,128)(2,1)S(1)}, bf16[960,1280]{1,0:T(8,128)(2,1)}, u32[]{:S(2)}) copy-start(bf16[960,1280]{1,0:T(8,128)(2,1)} %all-gather.22.cloned.1.call-done) | copy-start | bytes 7372804
  321.4 2.8 copy-start.39
  321.4 2.8 copy-start.41
  321.4 3.5 copy-start.34
  329.8 84.9 %reduce-scatter.6.cloned.1.call-start = ((), (), s32[]{:S(2)}) async-start(), calls=%async_computation.13 | async-start | bytes 2949120 | tf_op jit(solution)/shard_map/reduce_scatter | solution.py:187
  336.4 78.2 %copy-start.11 = (bf16[2,256,960]{1,2,0:T(8,128)(2,1)S(1)}, bf16[2,256,960]{1,2,0:T(8,128)(2,1)}, u32[]{:S(2)}) copy-start(bf16[2,256,960]{1,2,0:T(8,128)(2,1)} %param.17) | copy-start | bytes 2949124
  414.7 3.5 copy-start.37
  421.2 168.7 %reduce-scatter.14.cloned.1.call-start = ((), (), s32[]{:S(2)}) async-start(), calls=%async_computation.20 | async-start | bytes 2949120 | tf_op jit(solution)/shard_map/while/body/eval_jaxpr/reduce_scatter | solution.py:226
  445.3 2.9 copy-start.3
  448.2 2.9 copy-start.1
  461.3 2.9 copy-start.3
  464.2 2.9 copy-start.1
  477.4 2.9 copy-start.3
  480.3 2.9 copy-start.1
  493.4 2.9 copy-start.3
  496.3 2.9 copy-start.1
  509.5 2.9 copy-start.3
  512.4 2.9 copy-start.1
  518.7 71.2 %copy-start.14 = (f32[2,256,640]{1,2,0:T(8,128)S(1)}, f32[2,256,640]{1,2,0:T(8,128)}, u32[]{:S(2)}) copy-start(f32[2,256,640]{1,2,0:T(8,128)} %get-tuple-element.693) | copy-start | bytes 3932164 | tf_op jit(solution)/shard_map/while
  592.0 167.4 %reduce-scatter.14.cloned.1.call-start = ((), (), s32[]{:S(2)}) async-start(), calls=%async_computation.20 | async-start | bytes 2949120 | tf_op jit(solution)/shard_map/while/body/eval_jaxpr/reduce_scatter | solution.py:226
  616.1 2.9 copy-start.3
  619.1 2.9 copy-start.1
  632.2 2.9 copy-start.3
  635.1 2.9 copy-start.1
  648.2 2.9 copy-start.3
  651.2 2.9 copy-start.1
  664.3 2.9 copy-start.3
  667.2 2.9 copy-start.1
  680.3 2.9 copy-start.3
  683.3 2.9 copy-start.1
  689.5 69.9 %copy-start.14 = (f32[2,256,640]{1,2,0:T(8,128)S(1)}, f32[2,256,640]{1,2,0:T(8,128)}, u32[]{:S(2)}) copy-start(f32[2,256,640]{1,2,0:T(8,128)} %get-tuple-element.693) | copy-start | bytes 3932164 | tf_op jit(solution)/shard_map/while
  761.7 3.7 copy-start.7
  761.7 75.9 %reduce-scatter.12.cloned.1.call-start = ((), (), s32[]{:S(2)}) async-start(), calls=%async_computation.17 | async-start | bytes 6144000 | tf_op jit(solution)/shard_map/reduce_scatter | solution.py:286
  773.9 2.1 copy-start.13
  773.9 2.1 copy-start.29
  776.0 2.5 copy-start.24
  776.1 2.5 copy-start.25
  789.3 116.6 %reduce-scatter.10.cloned.1.call-start = ((), (), s32[]{:S(2)}) async-start(), calls=%async_computation.16 | async-start | bytes 9216000 | tf_op jit(solution)/shard_map/reduce_scatter | solution.py:289
  790.8 4.8 copy-start.36
  790.8 4.8 copy-start.42
  795.6 3.5 copy-start.40
  805.9 146.1 %all-reduce.11.cloned.1.call-start = ((), (), s32[]{:S(2)}) async-start(), calls=%async_computation.18 | async-start | bytes 2457600 | tf_op jit(solution)/shard_map/psum | solution.py:20
  837.6 115.1 %copy-start.19 = (bf16[2,256,15,64]{1,3,2,0:T(8,128)(2,1)S(1)}, bf16[2,256,15,64]{1,3,2,0:T(8,128)(2,1)}, u32[]{:S(2)}) copy-start(bf16[2,256,15,64]{1,3,2,0:T(8,128)(2,1)} %copy-done.18) | copy-start | bytes 2949124
  837.6 236.3 %all-reduce.13.cloned.1.call-start = ((), (), s32[]{:S(2)}) async-start(), calls=%async_computation.19 | async-start | bytes 6144000 | tf_op jit(solution)/shard_map/psum | solution.py:20
  952.7 2.9 copy-start.26
  952.7 2.9 copy-start.38
  955.6 2.6 copy-start.30
  955.6 32.2 %copy-start.8 = (f32[2,256,960]{1,2,0:T(8,128)S(1)}, f32[2,256,960]{1,2,0:T(8,128)}, u32[]{:S(2)}) copy-start(f32[2,256,960]{1,2,0:T(8,128)} %copy-done.6) | copy-start | bytes 5898244
  1075.9 2.2 copy-start.9
  (44 other events, 66.3 us)
Sparse Core Ops, SparseCore 0:
  9.6 20.4 all-gather.11
  31.6 21.8 all-gather.9
  56.3 86.2 all-gather.13
  144.0 20.0 all-gather.15
  165.4 31.5 all-gather.25
  198.5 24.7 all-gather.23
  224.8 24.5 all-gather.21
  251.5 31.6 all-gather.17
  284.7 24.6 all-gather.19
  329.9 51.9 reduce-scatter.7
  384.3 30.3 reduce-scatter.5
  518.8 71.0 reduce-scatter.13
  689.7 69.7 reduce-scatter.13
  789.4 48.1 reduce-scatter.11
  840.1 65.6 reduce-scatter.9
  908.0 43.9 all-reduce.10
  954.5 119.3 all-reduce.12
